TPU v7x, 128 devices: a whole 4x4x4 slice. The times are simulated.
128 devices in a mesh: region: 8 (over y, core), sub: 16 (over x, z).
Axes of the slice: x: 4, y: 4, z: 4, core: 2. Of those that a mesh axis runs over, the one named last changes fastest.
Arguments:
- orbitals: bfloat16 [512, 48, 2304], P(('region', 'sub')), may hold values from -6 to 6
- trial_set: bfloat16 [512, 48, 2304], P(('region', 'sub')), may hold values from -6 to 6
- own_slot: int32 [512], P(('region', 'sub')), may hold values from 0 to 3
- partner_route: int32 [512, 1], P(('region', 'sub')), may hold values from 0 to 16; in each aligned block of 4 rows (0 to 3, 4 to 7, ...) at most 2 rows name the same one
- partner_slot: int32 [512], P(('region', 'sub')), may hold values from 0 to 3
- offsets: int32 [512, 3], replicated, may hold values from 0 to 23
Outputs:
- fock_orbitals: bfloat16 [512, 48, 2304], P(('region', 'sub'))
- fock_trial: bfloat16 [512, 48, 2304], P(('region', 'sub'))
Inputs may be any that keep to these rules, and one draw needn't show every extreme that they name: `partner_route`: values below 16 name the device of the same region with that sub index; 16 names the device of the next region (after the last comes the first) with the same sub index. Among the 4 pairs of one device no value occurs more than 2 times, and some device has a value exactly 2 times.
All inputs are finite; a program needn't handle non-finite values.
Results may differ from a plain program's by a relative error of at most 0.0042.
Values may be sent and summed in bfloat16 or wider, within the bound.
No kernel may reach another device: no remote copies, remote signals or barrier semaphores. Data moves between devices by JAX's collectives and lax.ppermute only.
A program may use at most 192 MiB of HBM per device.

v0:
```python
import math

import jax
import jax.numpy as jnp
from jax import lax
from jax.sharding import PartitionSpec as P

CAP = 2


SCREEN = 0.5


def shifted(block, axis, distance):
    devices = range(lax.axis_size(axis))
    route = [((i - distance) % len(devices), i) for i in devices]
    return lax.ppermute(block, axis, route)


def shifter(displace, box_edge):
    row_ids = lax.broadcasted_iota(jnp.int32, (box_edge, box_edge), 0)
    col_ids = lax.broadcasted_iota(jnp.int32, (box_edge, box_edge), 1)
    return (col_ids == row_ids + displace).astype(jnp.bfloat16)


def hartley(box_edge):
    row_ids = lax.broadcasted_iota(jnp.int32, (box_edge, box_edge), 0)
    col_ids = lax.broadcasted_iota(jnp.int32, (box_edge, box_edge), 1)
    phases = (row_ids * col_ids % box_edge).astype(jnp.float32) * (2.0 * math.pi / box_edge)
    return jnp.cos(phases) + jnp.sin(phases)


def kernel_table(box_edge):
    wave_no = jnp.arange(box_edge).astype(jnp.float32)
    eigen = 4.0 * jnp.sin(math.pi * wave_no / box_edge) ** 2
    spectrum = eigen[:, None, None] + eigen[None, :, None] + eigen[None, None, :] + SCREEN
    return 4.0 * math.pi / spectrum / float(box_edge * box_edge * box_edge)


def shift_box(flat, displace):
    box_edge = flat.shape[0]
    cells = flat.reshape(box_edge, box_edge, box_edge)
    cells = jnp.einsum(
        "ia,abc->ibc", shifter(displace[0], box_edge), cells, preferred_element_type=jnp.float32
    ).astype(jnp.bfloat16)
    cells = jnp.einsum(
        "jb,abc->ajc", shifter(displace[1], box_edge), cells, preferred_element_type=jnp.float32
    ).astype(jnp.bfloat16)
    cells = jnp.einsum(
        "kc,abc->abk", shifter(displace[2], box_edge), cells, preferred_element_type=jnp.float32
    ).astype(jnp.bfloat16)
    return cells.reshape(box_edge, box_edge * box_edge)


def solve_box(density, green, hartley_matrix):
    box_edge = density.shape[0]
    cells = density.reshape(box_edge, box_edge, box_edge)
    highest = lax.Precision.HIGHEST
    for pass_no in range(2):
        cells = jnp.einsum("ia,abc->ibc", hartley_matrix, cells, precision=highest)
        cells = jnp.einsum("jb,abc->ajc", hartley_matrix, cells, precision=highest)
        cells = jnp.einsum("kc,abc->abk", hartley_matrix, cells, precision=highest)
        if pass_no == 0:
            cells = cells * green
    return cells.reshape(box_edge, box_edge * box_edge)


def per_device(orbitals, trial_set, own_slot, partner_route, partner_slot, offsets):
    n_sub = lax.axis_size("sub")
    n_region = lax.axis_size("region")
    region = lax.axis_index("region")
    sub_index = lax.axis_index("sub")
    orb_dev = orbitals.shape[0]
    box_edge = orbitals.shape[1]
    plane_size = orbitals.shape[2]
    pair_count = own_slot.shape[0]
    slot_count = (n_sub + 1) * CAP
    routes = partner_route[:, 0]
    row_order = lax.broadcasted_iota(jnp.int32, (pair_count, pair_count), 0)
    sooner = lax.broadcasted_iota(jnp.int32, (pair_count, pair_count), 1)
    same_route = (routes[:, None] == routes[None, :]) & (sooner < row_order)
    order_no = jnp.sum(same_route.astype(jnp.int32), axis=1)
    position = routes * CAP + order_no
    slot_hits = position[:, None] == jnp.arange(slot_count, dtype=jnp.int32)[None, :]
    wanted = jnp.sum(jnp.where(slot_hits, partner_slot[:, None] + 1, 0), axis=0) - 1
    giving = jnp.sum(jnp.where(slot_hits, own_slot[:, None] + 1, 0), axis=0) - 1
    asked_sub, mates_sub = (
        lax.all_to_all(
            wanted[: n_sub * CAP].reshape(n_sub, CAP),
            "sub",
            split_axis=0,
            concat_axis=0,
            tiled=True,
        ),
        lax.all_to_all(
            giving[: n_sub * CAP].reshape(n_sub, CAP),
            "sub",
            split_axis=0,
            concat_axis=0,
            tiled=True,
        ),
    )
    asked_region, mates_region = shifted(
        (wanted[n_sub * CAP :], giving[n_sub * CAP :]), "region", 1
    )
    asked_slots = jnp.concatenate([asked_sub.reshape(n_sub * CAP), asked_region])

    def travel(buffer, step_by):
        layers = buffer.shape[0]
        sub_part = buffer[:, : n_sub * CAP].reshape(layers, n_sub, CAP, box_edge, plane_size)
        sub_moved = lax.all_to_all(sub_part, "sub", split_axis=1, concat_axis=1, tiled=True)
        region_part = shifted(buffer[:, n_sub * CAP :], "region", step_by)
        return jnp.concatenate(
            [sub_moved.reshape(layers, n_sub * CAP, box_edge, plane_size), region_part], axis=1
        )

    owner_hits = (asked_slots[None, :] == jnp.arange(orb_dev, dtype=jnp.int32)[:, None]).astype(
        jnp.bfloat16
    )

    def collect(summed, outgoing):
        returned = travel(outgoing[None], 1)[0]
        return summed + jnp.einsum(
            "os,sxp->oxp", owner_hits, returned, preferred_element_type=jnp.float32
        )

    home_dev = region * n_sub + sub_index
    partner_dev = jnp.where(
        routes < n_sub, region * n_sub + routes, (region + 1) % n_region * n_sub + sub_index
    )
    first_ids = home_dev * orb_dev + own_slot
    second_ids = partner_dev * orb_dev + partner_slot
    displace_all = offsets[first_ids] - offsets[second_ids]
    green = kernel_table(box_edge)
    hartley_matrix = hartley(box_edge)
    empty_sums = jnp.zeros((orb_dev, box_edge, plane_size), jnp.float32)
    empty_out = jnp.zeros((slot_count, box_edge, plane_size), jnp.bfloat16)

    def near_first(pair_no, summed, boxes):
        own_index = own_slot[pair_no]
        displace = displace_all[pair_no]
        local_wide = orbitals[own_index].astype(jnp.float32)
        theirs = shift_box(boxes[position[pair_no]], displace).astype(jnp.float32)
        potential = solve_box(local_wide * theirs, green, hartley_matrix)
        near_one = lax.optimization_barrier((potential * theirs).astype(jnp.bfloat16))
        return (summed.at[own_index].add(near_one.astype(jnp.float32)), potential, local_wide)

    def near_second(pair_no, summed, boxes):
        own_index = own_slot[pair_no]
        displace = displace_all[pair_no]
        local_trial = trial_set[own_index].astype(jnp.float32)
        theirs = shift_box(boxes[position[pair_no]], displace).astype(jnp.float32)
        pot_near = solve_box(theirs * local_trial, green, hartley_matrix)
        near_two = lax.optimization_barrier((pot_near * theirs).astype(jnp.bfloat16))
        return summed.at[own_index].add(near_two.astype(jnp.float32))

    clipped = jnp.clip(asked_slots, 0, orb_dev - 1)
    picked = jnp.take(jnp.stack([orbitals, trial_set], axis=0), clipped, axis=1)
    filled = (asked_slots >= 0)[None, :, None, None]
    both_sets = travel(jnp.where(filled, picked, jnp.zeros_like(picked)), -1)
    first_boxes = both_sets[0]

    def first_pass(pair_no, running):
        summed, outgoing = running
        summed, potential, local_wide = near_first(pair_no, summed, first_boxes)
        far_one = shift_box((potential * local_wide).astype(jnp.bfloat16), -displace_all[pair_no])
        return (summed, outgoing.at[position[pair_no]].set(far_one))

    def second_pass(pair_no, running):
        summed, outgoing = running
        own_index = own_slot[pair_no]
        displace = displace_all[pair_no]
        summed = near_second(pair_no, summed, both_sets[0])
        local_wide = orbitals[own_index].astype(jnp.float32)
        their_trial = shift_box(both_sets[1, position[pair_no]], displace).astype(jnp.float32)
        pot_far = solve_box(local_wide * their_trial, green, hartley_matrix)
        far_two = shift_box((pot_far * local_wide).astype(jnp.bfloat16), -displace)
        return (summed, outgoing.at[position[pair_no]].set(far_two))

    sums_orb, out_orb = lax.fori_loop(0, pair_count, first_pass, (empty_sums, empty_out))
    sums_orb = collect(sums_orb, out_orb)
    sums_trial, out_trial = lax.fori_loop(0, pair_count, second_pass, (empty_sums, empty_out))
    sums_trial = collect(sums_trial, out_trial)
    return ((-sums_orb).astype(jnp.bfloat16), (-sums_trial).astype(jnp.bfloat16))


def solution(mesh):
    in_specs = (
        P(("region", "sub"), None, None),
        P(("region", "sub"), None, None),
        P(("region", "sub")),
        P(("region", "sub"), None),
        P(("region", "sub")),
        P(),
    )
    out_specs = (P(("region", "sub"), None, None), P(("region", "sub"), None, None))
    return jax.shard_map(
        per_device, mesh=mesh, in_specs=in_specs, out_specs=out_specs, check_vma=False
    )
```

profile of v0, /device:TPU:0, one launch (start us, length us, event | category | flops | bytes accessed | tf_op | source)
XLA Modules:
  0.0 1008.0 jit_solution(8248329012947757947)
XLA Ops:
  3.7 8.0 all-to-all-start
  13.3 5.8 all-to-all-done
  20.7 7.2 gather_fusion.2
  27.9 6.5 select_bitcast_fusion
  34.4 7.1 slice.316
  43.9 5.0 all-to-all-start.1
  53.4 245.4 %all-to-all-done.1 = bf16[2,16,2,48,2304]{4,3,0,2,1:T(8,128)(2,1)} async-done(((bf16[2,16,2,48,2304]{4,3,0,2,1:T(8,128)(2,1)}), bf16[2,16,2,48,2304]{4,3,0,2,1:T(8,128)(2,1)}, u32[]{:S(2)}, u32[]{:S(2)}) %all-to-all-start.1) | async-done | bytes 14155808 | tf_op jit(solution)/shard_map/all_to_all | solution.py:111
  298.8 6.8 copy.155
  305.6 6.4 pad_maximum_fusion
  312.0 3.1 copy-done
  315.6 3.5 broadcast_in_dim.77.clone.1
  320.6 292.3 %while.39 = (s32[]{:T(128)}, f32[4,48,2304]{2,0,1:T(4,128)}, bf16[34,48,2304]{2,1,0:T(8,128)(2,1)}, s32[4]{0:T(128)S(1)}, s32[4,3]{1,0:T(4,128)S(1)}, /*index=5*...) while((s32[]{:T(128)}, f32[4,48,2304]{2,0,1:T(4,128)}, ...), condition=%wide.region_9.10_spmd.clone.clone, body=%wide.region_6.9_spmd.clone.clone.sunk | while | flops 864021120 | bytes 43896580 | solution.py:182
  377.6 3.6 slice.363
  401.5 8.2 scatter-add.17
  443.6 3.6 slice.363
  467.5 8.2 scatter-add.17
  509.6 3.6 slice.363
  533.5 8.2 scatter-add.17
  575.6 3.6 slice.363
  599.6 8.2 scatter-add.17
  612.9 9.2 copy.233
  622.0 6.4 slice.322
  628.4 14.6 %reshape.502 = bf16[1,16,2,48,2304]{4,2,1,3,0:T(2,128)(2,1)} reshape(bf16[1,32,48,2304]{3,1,2,0:T(8,128)(2,1)} %slice.322) | data formatting | bytes 14155776 | tf_op jit(solution)/shard_map/reshape | solution.py:110
  643.0 7.4 copy.162
  650.4 9.5 all-to-all-start.3
  660.0 6.7 fusion.181
  666.7 3.5 broadcast_in_dim.77.clone
  671.6 176.5 %while.38 = (s32[]{:T(128)}, f32[4,48,2304]{2,0,1:T(4,128)}, bf16[34,48,2304]{2,1,0:T(8,128)(2,1)}, s32[4]{0:T(128)S(1)}, bf16[4,48,2304]{2,1,0:T(8,128)(2,1)}, ...) while((s32[]{:T(128)}, f32[4,48,2304]{2,0,1:T(4,128)}, ...), condition=%wide.region_5.6_spmd.clone.clone, body=%wide.region_2.5_spmd.clone.clone.sunk | while | flops 448603008 | bytes 19073856 | solution.py:180
  688.6 2.9 convolution_multiply_fusion.7
  707.8 8.2 scatter-add.16
  732.6 2.9 convolution_multiply_fusion.7
  751.8 8.2 scatter-add.16
  776.5 2.9 convolution_multiply_fusion.7
  795.8 8.2 scatter-add.16
  820.5 2.9 convolution_multiply_fusion.7
  839.8 8.2 scatter-add.16
  848.1 9.2 copy.234
  857.3 6.3 slice.320
  863.6 14.6 %reshape.500 = bf16[1,16,2,48,2304]{4,2,1,3,0:T(2,128)(2,1)} reshape(bf16[1,32,48,2304]{3,1,2,0:T(8,128)(2,1)} %slice.320) | data formatting | bytes 14155776 | tf_op jit(solution)/shard_map/reshape | solution.py:110
  878.2 7.4 copy.158
  885.6 7.3 all-to-all-start.2
  897.3 7.4 copy.163
  904.7 15.1 %reshape.503 = bf16[1,32,48,2304]{3,1,2,0:T(8,128)(2,1)} reshape(bf16[1,16,2,48,2304]{4,2,1,3,0:T(2,128)(2,1)} %copy.163) | data formatting | bytes 14155776 | tf_op jit(solution)/shard_map/reshape | solution.py:114
  919.9 5.1 fusion.177
  926.5 52.1 %all-to-all-done.2 = bf16[1,16,2,48,2304]{4,2,3,0,1:T(2,128)(2,1)} async-done(((bf16[1,16,2,48,2304]{4,2,3,0,1:T(2,128)(2,1)}), bf16[1,16,2,48,2304]{4,2,3,0,1:T(2,128)(2,1)}, u32[]{:S(2)}, u32[]{:S(2)}) %all-to-all-start.2) | async-done | bytes 7077920 | tf_op jit(solution)/shard_map/all_to_all | solution.py:111
  978.6 7.4 copy.159
  986.0 15.1 %reshape.501 = bf16[1,32,48,2304]{3,1,2,0:T(8,128)(2,1)} reshape(bf16[1,16,2,48,2304]{4,2,1,3,0:T(2,128)(2,1)} %copy.159) | data formatting | bytes 14155776 | tf_op jit(solution)/shard_map/reshape | solution.py:114
  1001.1 5.1 fusion.174
  (542 shorter events, 339.7 us)
Async XLA Ops:
  3.7 15.5 %all-to-all-start = ((s32[16,1,2]{2,1,0:T(1,128)}), s32[16,1,2]{2,1,0:T(1,128)S(1)}, u32[]{:S(2)}, u32[]{:S(2)}) async-start(s32[16,1,2]{2,1,0:T(1,128)} %bitcast.3), calls=%async_computation | async-start | bytes 16384 | tf_op jit(solution)/shard_map/all_to_all | solution.py:88
  11.7 7.5 collective-permute-start
  34.4 9.5 copy-start.1
  43.9 254.8 %all-to-all-start.1 = ((bf16[2,16,2,48,2304]{4,3,0,2,1:T(8,128)(2,1)}), bf16[2,16,2,48,2304]{4,3,0,2,1:T(8,128)(2,1)}, u32[]{:S(2)}, u32[]{:S(2)}) async-start(bf16[2,16,2,48,2304]{4,3,0,2,1:T(8,128)(2,1)} %bitcast.403), calls=%async_computation.1 | async-start | bytes 28311552 | tf_op jit(solution)/shard_map/all_to_all | solution.py:111
  50.2 255.3 %collective-permute-start.1 = (bf16[2,2,48,2304]{3,2,0,1:T(8,128)(2,1)S(1)}, bf16[2,2,48,2304]{3,2,0,1:T(8,128)(2,1)S(1)}, u32[]{:S(2)}, u32[]{:S(2)}) collective-permute-start(bf16[2,2,48,2304]{3,2,0,1:T(8,128)(2,1)S(1)} %slice.317), channel_id=1, source_target_pairs={{16,0},{32,16},{48,32},{64,48},{80,64},{96,80},{112,96},{0,112},{1... | collective-permute-start | bytes 2654216 | tf_op jit(solution)/shard_map/ppermute | solution.py:17
  305.5 9.5 copy-start
  305.6 10.1 copy-start.5
  400.4 9.3 copy-start.13
  400.4 9.3 copy-start.19
  400.4 9.3 copy-start.25
  400.4 9.3 copy-start.29
  466.4 9.3 copy-start.13
  466.4 9.3 copy-start.19
  466.4 9.3 copy-start.25
  466.4 9.3 copy-start.29
  532.4 9.3 copy-start.13
  532.4 9.3 copy-start.19
  532.4 9.3 copy-start.25
  532.4 9.3 copy-start.29
  598.4 9.3 copy-start.13
  598.4 9.3 copy-start.19
  598.4 9.3 copy-start.25
  598.4 9.3 copy-start.29
  650.4 9.5 copy-start.6
  650.4 235.2 %all-to-all-start.3 = ((bf16[1,16,2,48,2304]{4,2,3,0,1:T(2,128)(2,1)}), bf16[1,16,2,48,2304]{4,2,3,0,1:T(2,128)(2,1)}, u32[]{:S(2)}, u32[]{:S(2)}) async-start(bf16[1,16,2,48,2304]{4,2,3,0,1:T(2,128)(2,1)} %copy.162), calls=%async_computation.3 | async-start | bytes 14155776 | tf_op jit(solution)/shard_map/all_to_all | solution.py:111
  706.7 9.3 copy-start.21
  706.7 9.3 copy-start.27
  706.7 9.3 copy-start.31
  716.0 8.8 copy-start.20
  716.0 8.8 copy-start.26
  716.0 8.8 copy-start.30
  750.7 9.3 copy-start.21
  750.7 9.3 copy-start.27
  750.7 9.3 copy-start.31
  760.0 8.7 copy-start.20
  794.7 9.3 copy-start.21
  794.7 9.3 copy-start.27
  794.7 9.3 copy-start.31
  804.0 8.8 copy-start.20
  804.0 8.8 copy-start.26
  804.0 8.8 copy-start.30
  838.7 9.3 copy-start.21
  838.7 9.3 copy-start.27
  838.7 9.3 copy-start.31
  885.6 93.0 %all-to-all-start.2 = ((bf16[1,16,2,48,2304]{4,2,3,0,1:T(2,128)(2,1)}), bf16[1,16,2,48,2304]{4,2,3,0,1:T(2,128)(2,1)}, u32[]{:S(2)}, u32[]{:S(2)}) async-start(bf16[1,16,2,48,2304]{4,2,3,0,1:T(2,128)(2,1)} %copy.158), calls=%async_computation.2 | async-start | bytes 14155776 | tf_op jit(solution)/shard_map/all_to_all | solution.py:111
  894.6 25.3 %collective-permute-start.3 = (bf16[1,2,48,2304]{3,1,2,0:T(2,128)(2,1)S(1)}, bf16[1,2,48,2304]{3,1,2,0:T(2,128)(2,1)S(1)}, u32[]{:S(2)}, u32[]{:S(2)}) collective-permute-start(bf16[1,2,48,2304]{3,1,2,0:T(2,128)(2,1)S(1)} %slice.323), channel_id=1, source_target_pairs={{112,0},{0,16},{16,32},{32,48},{48,64},{64,80},{80,96},{96,112},{1... | collective-permute-start | bytes 1327112 | tf_op jit(solution)/shard_map/ppermute | solution.py:17
  896.3 104.8 %collective-permute-start.2 = (bf16[1,2,48,2304]{3,1,2,0:T(2,128)(2,1)S(1)}, bf16[1,2,48,2304]{3,1,2,0:T(2,128)(2,1)S(1)}, u32[]{:S(2)}, u32[]{:S(2)}) collective-permute-start(bf16[1,2,48,2304]{3,1,2,0:T(2,128)(2,1)S(1)} %slice.321), channel_id=1, source_target_pairs={{112,0},{0,16},{16,32},{32,48},{48,64},{64,80},{80,96},{96,112},{1... | collective-permute-start | bytes 1327112 | tf_op jit(solution)/shard_map/ppermute | solution.py:17
  904.7 15.1 %copy-start.23 = (s32[34]{0:T(128)S(1)}, s32[34]{0:T(128)}, u32[]{:S(2)}) copy-start(s32[34]{0:T(128)} %copy-done.22) | copy-start | bytes 412
  (52 other events, 163.4 us)
where the time goes:
time: 1020 us; the launch traced here: 1010 us
  local copies, waits for them, and re-layouts  335 us (33%)
  waiting for transfers between devices  303 us (30%)
  matrix products  179 us (18%)
  other arithmetic  96 us (9%)
  loops' own time  61.7 us (6%)
  starting transfers between devices  31.9 us (3%)
    all_to_all x3, waiting for transfers between devices, travel(): lax.all_to_all(sub_part, 'sub', split_axis=1, concat_axis=1, tiled=True)  297 us
    dot_general x24, matrix products, solve_box(): cells = jnp.einsum('kc,abc->abk', hartley_matrix, cells, precision=highest)  59.1 us
    dot_general x24, matrix products, solve_box(): cells = jnp.einsum('ia,abc->ibc', hartley_matrix, cells, precision=highest)  53.3 us
    another operation x1, loops' own time, per_device(): lax.fori_loop(0, pair_count, second_pass, (empty_sums, empty_out))  44.4 us
    reshape x4, local copies, waits for them, and re-layouts, travel(): buffer[:, :n_sub * CAP].reshape(layers, n_sub, CAP, box_edge, plane_size)  44 us
    scatter-add x8, local copies, waits for them, and re-layouts, near_second(): return summed.at[own_index].add(near_two.astype(jnp.float32))  34.5 us
    scatter-add x8, local copies, waits for them, and re-layouts, near_first(): summed.at[own_index].add(near_one.astype(jnp.float32))  34.5 us
    reshape x2, local copies, waits for them, and re-layouts, travel(): sub_moved.reshape(layers, n_sub * CAP, box_edge, plane_size)  30.2 us
  transfers between devices with their start and end apart: 8, of which 3 were waited for; matrix products, arithmetic and copies ran while one was open for 27% of the time, Pallas kernels for 0%

commit v1 on v0

v1 whole, which is shorter than its diff:
```python
import math

import jax
import jax.numpy as jnp
import ml_dtypes
import numpy as np
from jax import lax
from jax.experimental import pallas as pl
from jax.experimental.pallas import tpu as pltpu
from jax.sharding import PartitionSpec as P

BOX = 48
PLANE = BOX * BOX
CHUNK = PLANE // 6
SCREEN = 0.5
GRID = 4
N_SUB = GRID * GRID
ORB_DEV = 4
PAIRS_DEV = 4
N_PAIRS = N_SUB * PAIRS_DEV

PLACES = ((0, 0), (0, 1), (1, 0), (1, 1), (1, 3), (3, 1))
REGION_SOURCE = len(PLACES)
SOURCES = len(PLACES) + 1
LIST_WIDTH = 8

HALF_ROOT3 = math.sqrt(3.0) / 2.0
F32 = jnp.float32
BF16 = jnp.bfloat16


def meeting_table():
    found = [[] for _ in range(N_SUB)]
    for i, (ax, az) in enumerate(PLACES):
        for j, (bx, bz) in enumerate(PLACES):
            delta = (ax - bx) % GRID * GRID + (az - bz) % GRID
            found[delta].append(i + 8 * j + 64 * ax + 512 * az)
    most = max(len(f) for f in found)
    codes = np.array([f + [f[-1]] * (most - len(f)) for f in found], np.int32)
    counts = np.array([len(f) for f in found], np.int32)
    return np.concatenate([counts, codes.reshape(-1)]), most


def high_low(matrix):
    high = matrix.astype(ml_dtypes.bfloat16)
    low = (matrix - high.astype(np.float64)).astype(ml_dtypes.bfloat16)
    return np.stack([high, low])


def cas(angles):
    return np.cos(angles) + np.sin(angles)


def transform_tables():
    turn = 2.0 * math.pi / BOX
    n = np.arange(BOX)
    line = cas(turn * (n[:, None] * n[None, :] % BOX))
    q = np.arange(8)[:, None]
    m = np.arange(8)[None, :]

    def real_part(j):
        return np.kron(cas(turn * (q * (6 * m + j) % BOX)), line)

    def complex_part(j):
        angle = turn * (q * (6 * m + j) % BOX)
        c, s = np.cos(angle), np.sin(angle)
        return np.kron(np.block([[c, -s], [s, c]]), line)

    small = np.stack([real_part(0), real_part(3)])
    large = np.stack([complex_part(1), complex_part(2)])
    lam = 4.0 * np.sin(math.pi * n / BOX) ** 2

    def spectrum(j, weight):
        ky = 6 * np.arange(8) + j
        total = lam[:, None, None] + lam[ky][None, :, None] + lam[None, None, :] + SCREEN
        return (weight * 4.0 * math.pi / total / float(BOX**3)).reshape(BOX, CHUNK)

    one, two = spectrum(1, 2.0), spectrum(2, 2.0)
    green = np.concatenate([spectrum(0, 1.0), spectrum(3, 1.0), one, one, two, two], axis=1)
    rows = high_low(line)
    rows = np.concatenate([rows[0], rows[1], rows[0]], axis=1)
    return dict(
        small=high_low(small),
        large=high_low(large),
        small_back=high_low(small.transpose(0, 2, 1)),
        large_back=high_low(large.transpose(0, 2, 1)),
        green=green.astype(np.float32),
        rows=rows,
    )


def plan_kernel(most, where, meta, offsets, table, listing, loads):
    region, sub, n_region = where[0], where[1], where[2]
    sign = 1 - 2 * (region & 1)
    next_region = jnp.where(region + 1 == n_region, 0, region + 1)
    for i in range(N_SUB):
        loads[i] = 0
    listing[0] = 0

    def place(pair, turn):
        home = pair >> 2
        lane = pair & 3
        own_slot = meta[home * 12 + lane]
        route = meta[home * 12 + 4 + lane]
        partner_slot = meta[home * 12 + 8 + lane]
        abroad = route == N_SUB
        other = jnp.where(abroad, home, route)
        hx, hz = home >> 2, home & 3
        dx = (sign * ((other >> 2) - hx)) & 3
        dz = (sign * ((other & 3) - hz)) & 3
        delta = dx * GRID + dz
        count = jnp.where(abroad, 1, table[delta])
        mine_now = jnp.where(count == 1, 0, 1) == turn

        @pl.when(mine_now)
        def _():
            best_load = jnp.int32(1 << 20)
            best_code = jnp.int32(0)
            best_dev = home
            for k in range(most):
                code = table[N_SUB + delta * most + k]
                sx, sz = (code >> 6) & 7, (code >> 9) & 7
                dev = ((hx + sign * sx) & 3) * GRID + ((hz + sign * sz) & 3)
                load = loads[dev]
                better = load < best_load
                best_load = jnp.where(better, load, best_load)
                best_code = jnp.where(better, code, best_code)
                best_dev = jnp.where(better, dev, best_dev)
            dev = jnp.where(abroad, home, best_dev)
            loads[dev] = loads[dev] + 1

            @pl.when(dev == sub)
            def _():
                at = listing[0]
                listing[0] = at + 1
                row = (at + 1) * LIST_WIDTH
                first = (region * N_SUB + home) * ORB_DEV + own_slot
                second_region = jnp.where(abroad, next_region, region)
                second = (second_region * N_SUB + other) * ORB_DEV + partner_slot
                listing[row] = jnp.where(abroad, 0, best_code & 7)
                listing[row + 1] = own_slot
                listing[row + 2] = jnp.where(abroad, REGION_SOURCE, (best_code >> 3) & 7)
                listing[row + 3] = partner_slot
                for c in range(3):
                    listing[row + 4 + c] = offsets[first * 3 + c] - offsets[second * 3 + c]

    for turn in range(2):

        def body(pair, carry, turn=turn):
            place(pair, turn)
            return carry

        lax.fori_loop(0, N_PAIRS, body, 0)


def split_store(high_ref, low_ref, rows, lanes, value):
    high = value.astype(BF16)
    high_ref[rows, lanes] = high
    low_ref[rows, lanes] = (value - high.astype(F32)).astype(BF16)


def three_dots(high, low, weights, index, columns):
    w_high = weights[0, index, :, columns]
    w_low = weights[1, index, :, columns]
    total = jnp.dot(high, w_high, preferred_element_type=F32)
    total += jnp.dot(low, w_high, preferred_element_type=F32)
    return total + jnp.dot(high, w_low, preferred_element_type=F32)


def solve(density, high, low, work, small, large, small_back, large_back, green, rows, boxes):
    groups = ((0, 0), (0, 1), (1, 0), (1, 1))
    starts = (0, CHUNK, 2 * CHUNK, 4 * CHUNK)
    for b in range(boxes):
        at = pl.ds(b * BOX, BOX)
        for c in range(CHUNK // 128):
            x = [density(b, pl.ds(r * CHUNK + c * 128, 128)) for r in range(6)]
            u = [x[r] + x[r + 3] for r in range(3)]
            v = [x[r] - x[r + 3] for r in range(3)]
            parts = (
                u[0] + u[1] + u[2],
                v[0] - v[1] + v[2],
                v[0] + 0.5 * (v[1] - v[2]),
                -HALF_ROOT3 * (v[1] + v[2]),
                u[0] - 0.5 * (u[1] + u[2]),
                -HALF_ROOT3 * (u[1] - u[2]),
            )
            for j, part in enumerate(parts):
                split_store(high, low, at, pl.ds(j * CHUNK + c * 128, 128), part)

    def plane_pass(small_w, large_w):
        for (is_large, index), start in zip(groups, starts):
            depth = 2 * CHUNK if is_large else CHUNK
            weights = large_w if is_large else small_w
            h = high[:, pl.ds(start, depth)]
            l = low[:, pl.ds(start, depth)]
            for c in range(depth // CHUNK):
                work[:, pl.ds(start + c * CHUNK, CHUNK)] = three_dots(
                    h, l, weights, index, pl.ds(c * CHUNK, CHUNK)
                )

    plane_pass(small, large)

    def row_pass(value):
        h = value.astype(BF16)
        l = (value - h.astype(F32)).astype(BF16)
        return jnp.dot(
            rows[...], jnp.concatenate([h, h, l], axis=0), preferred_element_type=F32
        )

    for b in range(boxes):
        at = pl.ds(b * BOX, BOX)
        for c in range(PLANE // 256):
            lanes = pl.ds(c * 256, 256)
            waves = row_pass(work[at, lanes]) * green[:, lanes]
            split_store(high, low, at, lanes, row_pass(waves))

    plane_pass(small_back, large_back)
    for b in range(boxes):
        at = pl.ds(b * BOX, BOX)
        for c in range(CHUNK // 128):
            t0, t3, t1r, t1i, t2r, t2i = [
                work[at, pl.ds(j * CHUNK + c * 128, 128)] for j in range(6)
            ]
            a0 = t0 + t2r
            t2h = t0 - 0.5 * t2r
            a1 = t2h - HALF_ROOT3 * t2i
            a2 = t2h + HALF_ROOT3 * t2i
            t1s = HALF_ROOT3 * t1i
            b0 = t3 + t1r
            b1 = 0.5 * t1r - t3 - t1s
            b2 = t3 - 0.5 * t1r - t1s
            values = (a0 + b0, a1 + b1, a2 + b2, a0 - b0, a1 - b1, a2 - b2)
            for r, value in enumerate(values):
                work[at, pl.ds(r * CHUNK + c * 128, 128)] = value


def shift_box(value, dx, dy, dz):
    steps = dy * BOX + dz
    value = pltpu.roll(value, jnp.where(dx > 0, BOX - dx, -dx), 0)
    value = pltpu.roll(value, jnp.where(steps > 0, PLANE - steps, -steps), 1)
    lane = lax.broadcasted_iota(jnp.int32, (1, PLANE), 1)
    y = (lane * 43691) >> 21
    z = lane - BOX * y
    x = lax.broadcasted_iota(jnp.int32, (BOX, 1), 0)

    def inside(place, step):
        return ((place + step >= 0) & (place + step < BOX)).astype(F32)

    keep = inside(y, dy) * inside(z, dz)
    return jnp.where(inside(x, dx) * keep > 0.5, value, 0.0)


def rounded(value):
    return value.astype(BF16).astype(F32)


def exchange_kernel(second, *refs):
    sets = 2 if second else 1
    listing = refs[0]
    refs = refs[1:]
    n_in = sets * (SOURCES + 1)
    boxes_in = refs[:n_in]
    small, large, small_back, large_back, green, rows = refs[n_in : n_in + 6]
    outs = refs[n_in + 6 : n_in + 6 + SOURCES + 1]
    acc, held, theirs, high, low, work, sems = refs[n_in + 6 + SOURCES + 1 :]
    per_step = 1 if second else 2
    loads_per_step = 4 if second else 4
    count = listing[0]
    steps = (count + per_step - 1) // per_step

    def fetch(group, source, slot, target, sem):
        refs_of = boxes_in[group * (SOURCES + 1) : (group + 1) * (SOURCES + 1)]
        for s in range(SOURCES):
            if s == 3:
                for half in range(2):

                    @pl.when((source == s) & ((slot >> 1) == half))
                    def _(half=half):
                        pltpu.make_async_copy(
                            refs_of[3 + half].at[slot & 1], target, sem
                        ).start()
            else:
                at = s if s < 3 else s + 1

                @pl.when(source == s)
                def _(at=at):
                    pltpu.make_async_copy(refs_of[at].at[slot], target, sem).start()

    def wanted(step, i):
        if second:
            row = (step + 1) * LIST_WIDTH
            side = i & 1
            return i >> 1, listing[row + 2 * side], listing[row + 2 * side + 1], None
        pair = step * 2 + (i >> 1)
        row = (pair + 1) * LIST_WIDTH
        side = i & 1
        return 0, listing[row + 2 * side], listing[row + 2 * side + 1], pair < count

    def start_loads(step, buffer):
        for i in range(loads_per_step):
            group, source, slot, there = wanted(step, i)
            if there is None:
                fetch(group, source, slot, held.at[buffer, i], sems.at[buffer, i])
            else:

                @pl.when(there)
                def _():
                    fetch(group, source, slot, held.at[buffer, i], sems.at[buffer, i])

    def wait_loads(step, buffer):
        for i in range(loads_per_step):
            there = wanted(step, i)[3]

            def wait():
                pltpu.make_async_copy(
                    boxes_in[0].at[0], held.at[buffer, i], sems.at[buffer, i]
                ).wait()

            if there is None:
                wait()
            else:
                pl.when(there)(wait)

    @pl.when(steps > 0)
    def _():
        start_loads(0, 0)

    def clear(i, carry):
        acc[i] = jnp.zeros((BOX, PLANE), F32)
        return carry

    lax.fori_loop(0, SOURCES * ORB_DEV, clear, 0)

    def add(source, slot, value):
        at = source * ORB_DEV + slot
        acc[at] = acc[at] + value

    def one_step(step, carry):
        buffer = step & 1

        @pl.when(step + 1 < steps)
        def _():
            start_loads(step + 1, 1 - buffer)

        wait_loads(step, buffer)
        consts = (small, large, small_back, large_back, green, rows)
        if second:
            row = (step + 1) * LIST_WIDTH
            dx, dy, dz = listing[row + 4], listing[row + 5], listing[row + 6]
            theirs[0] = shift_box(held[buffer, 1].astype(F32), dx, dy, dz)
            theirs[1] = shift_box(held[buffer, 3].astype(F32), dx, dy, dz)

            def density(b, lanes):
                mine = held[buffer, 2 - 2 * b, :, lanes].astype(F32)
                return mine * theirs[b, :, lanes]

            solve(density, high, low, work, *consts, 2)
            near = rounded(work[pl.ds(0, BOX), :] * theirs[0])
            add(listing[row], listing[row + 1], near)
            far = rounded(work[pl.ds(BOX, BOX), :] * held[buffer, 0].astype(F32))
            add(listing[row + 2], listing[row + 3], shift_box(far, -dx, -dy, -dz))
        else:
            for i in range(2):
                row = (step * 2 + i + 1) * LIST_WIDTH

                @pl.when(step * 2 + i < count)
                def _(i=i, row=row):
                    theirs[i] = shift_box(
                        held[buffer, 2 * i + 1].astype(F32),
                        listing[row + 4],
                        listing[row + 5],
                        listing[row + 6],
                    )

            def density(b, lanes):
                return held[buffer, 2 * b, :, lanes].astype(F32) * theirs[b, :, lanes]

            solve(density, high, low, work, *consts, 2)
            for i in range(2):
                row = (step * 2 + i + 1) * LIST_WIDTH

                @pl.when(step * 2 + i < count)
                def _(i=i, row=row):
                    potential = work[pl.ds(i * BOX, BOX), :]
                    add(listing[row], listing[row + 1], rounded(potential * theirs[i]))
                    far = rounded(potential * held[buffer, 2 * i].astype(F32))
                    far = shift_box(far, -listing[row + 4], -listing[row + 5], -listing[row + 6])
                    add(listing[row + 2], listing[row + 3], far)

        return carry

    lax.fori_loop(0, steps, one_step, 0)

    sizes = (4, 4, 4, 2, 2, 4, 4, 4)
    at = 0
    for out, size in zip(outs, sizes):

        def put(i, carry, out=out, at=at):
            out[i] = acc[at + i].astype(out.dtype)
            return carry

        lax.fori_loop(0, size, put, 0)
        at += size


def exchange(second, listing, boxes, tables):
    sizes = (4, 4, 4, 2, 2, 4, 4, 4)
    any_space = pl.BlockSpec(memory_space=pl.ANY)
    vmem = pl.BlockSpec(memory_space=pltpu.VMEM)
    smem = pl.BlockSpec(memory_space=pltpu.SMEM)
    outs = [
        jax.ShapeDtypeStruct((size, BOX, PLANE), F32 if i == 0 else BF16)
        for i, size in enumerate(sizes)
    ]

    def kernel(*refs):
        exchange_kernel(second, *refs)

    return pl.pallas_call(
        kernel,
        out_shape=outs,
        in_specs=[smem] + [any_space] * len(boxes) + [vmem] * len(tables),
        out_specs=[vmem] * len(outs),
        scratch_shapes=[
            pltpu.VMEM((SOURCES * ORB_DEV, BOX, PLANE), F32),
            pltpu.VMEM((2, 4, BOX, PLANE), BF16),
            pltpu.VMEM((2, BOX, PLANE), F32),
            pltpu.VMEM((2 * BOX, PLANE), BF16),
            pltpu.VMEM((2 * BOX, PLANE), BF16),
            pltpu.VMEM((2 * BOX, PLANE), F32),
            pltpu.SemaphoreType.DMA((2, 4)),
        ],
        compiler_params=pltpu.CompilerParams(vmem_limit_bytes=56 * 1024 * 1024),
        cost_estimate=pl.CostEstimate(
            flops=(2 if second else 1) * 10_000_000_000,
            bytes_accessed=30_000_000,
            transcendentals=0,
        ),
        name="second_application" if second else "first_application",
    )(listing, *boxes, *tables)


def moves(n_region):
    def step(dx, dz):
        pairs = []
        for region in range(n_region):
            sign = 1 - 2 * (region % 2)
            for x in range(GRID):
                for z in range(GRID):
                    to = (x + sign * dx) % GRID * GRID + (z + sign * dz) % GRID
                    pairs.append((region * N_SUB + x * GRID + z, region * N_SUB + to))

        def move(block):
            return lax.ppermute(block, ("region", "sub"), pairs)

        return move

    def across(distance):
        pairs = [(i, (i + distance) % n_region) for i in range(n_region)]

        def move(block):
            return lax.ppermute(block, "region", pairs)

        return move

    return step, across


def per_device(orbitals, trial_set, own_slot, partner_route, partner_slot, offsets):
    n_region = lax.axis_size("region")
    region = lax.axis_index("region")
    sub = lax.axis_index("sub")
    step, across = moves(n_region)
    tables = transform_tables()
    tables = [
        jnp.asarray(tables[k])
        for k in ("small", "large", "small_back", "large_back", "green", "rows")
    ]
    table, most = meeting_table()
    meta = jnp.concatenate([own_slot, partner_route[:, 0], partner_slot])
    meta = lax.all_gather(meta, "sub").reshape(-1)
    where = jnp.stack([region, sub, jnp.int32(n_region)]).astype(jnp.int32)
    smem = pl.BlockSpec(memory_space=pltpu.SMEM)

    def planner(*refs):
        plan_kernel(most, *refs)

    listing = pl.pallas_call(
        planner,
        out_shape=jax.ShapeDtypeStruct(((N_PAIRS + 1) * LIST_WIDTH,), jnp.int32),
        in_specs=[smem] * 4,
        out_specs=smem,
        scratch_shapes=[pltpu.SMEM((N_SUB,), jnp.int32)],
        name="plan",
    )(where, meta, offsets.reshape(-1), jnp.asarray(table))

    def spread(boxes):
        b01 = step(0, 1)(boxes)
        b10 = step(1, 0)(boxes)
        abroad = across(-1)(boxes)
        b13 = step(0, -1)(b10)
        b31 = step(-1, 0)(b01)
        b11_low = step(1, 0)(b01[:2])
        b11_high = step(0, 1)(b10[2:])
        return [boxes, b01, b10, b11_low, b11_high, b13, b31, abroad]

    def gather_back(parts):
        own, c01, c10, c11_low, c11_high, c13, c31, c_abroad = parts
        r13 = step(0, 1)(c13)
        r31 = step(1, 0)(c31)
        r11_low = step(-1, 0)(c11_low)
        r11_high = step(0, -1)(c11_high)
        r_abroad = across(1)(c_abroad)
        none = jnp.zeros_like(r11_low)
        m01 = (
            c01.astype(F32) + r31.astype(F32) + jnp.concatenate([r11_low, none]).astype(F32)
        ).astype(BF16)
        m10 = (
            c10.astype(F32) + r13.astype(F32) + jnp.concatenate([none, r11_high]).astype(F32)
        ).astype(BF16)
        f01 = step(0, -1)(m01)
        f10 = step(-1, 0)(m10)
        total = own + r_abroad.astype(F32) + f01.astype(F32) + f10.astype(F32)
        return (-total).astype(BF16)

    orbital_boxes = spread(orbitals)
    trial_boxes = spread(trial_set)
    first = exchange(False, listing, orbital_boxes, tables)
    second = exchange(True, listing, orbital_boxes + trial_boxes, tables)
    return gather_back(first), gather_back(second)


def solution(mesh):
    in_specs = (
        P(("region", "sub"), None, None),
        P(("region", "sub"), None, None),
        P(("region", "sub")),
        P(("region", "sub"), None),
        P(("region", "sub")),
        P(),
    )
    out_specs = (P(("region", "sub"), None, None), P(("region", "sub"), None, None))
    return jax.shard_map(
        per_device, mesh=mesh, in_specs=in_specs, out_specs=out_specs, check_vma=False
    )
```

time: 1020 us -> 190 us (0.19); the launches traced: 1010 us -> 189 us
  local copies, waits for them, and re-layouts: 335 us -> 3.52 us
  waiting for transfers between devices: 303 us -> 42 us
  matrix products: 179 us -> 0 us
  other arithmetic: 96 us -> 4.6 us
  loops' own time: 61.7 us -> 0 us
  Pallas kernels: 0 us -> 58.6 us
  starting transfers between devices: 31.9 us -> 59.7 us
  blocking collectives: 0 us -> 18.7 us
    all_to_all x4 -> x0, waiting for transfers between devices: 303 us -> none  [the longest x3 297 us: travel(): lax.all_to_all(sub_part, 'sub', split_axis=1, concat_axis=1, tiled=True)]
    dot_general x114 -> x0, matrix products: 179 us -> none  [the longest x24 59.1 us: solve_box(): cells = jnp.einsum('kc,abc->abk', hartley_matrix, cells, precision=highest)]
    reshape x6 -> x1, local copies, waits for them, and re-layouts: 74.2 us -> 0.81 us  [per_device(): offsets.reshape(-1)]
    scatter-add x16 -> x0, local copies, waits for them, and re-layouts: 69.1 us -> none  [the longest x8 34.5 us: near_second(): return summed.at[own_index].add(near_two.astype(jnp.float32))]
    another operation x2 -> x0, loops' own time: 61.7 us -> none  [the longest x1 44.4 us: per_device(): lax.fori_loop(0, pair_count, second_pass, (empty_sums, empty_out))]
    pallas_call x0 -> x3, Pallas kernels: none -> 58.6 us  [the longest x2 50.3 us: exchange(): pl.pallas_call(kernel, out_shape=outs, in_specs=[smem] + [any_space] * le...]
    ppermute x4 -> x28, starting transfers between devices: 2.13 us -> 59.7 us  [the longest x24 55.3 us: move(): return lax.ppermute(block, ('region', 'sub'), pairs)]
    slice x23 -> x4, local copies, waits for them, and re-layouts: 46.8 us -> 1.13 us  [the longest x2 1.07 us: spread(): b11_low = step(1, 0)(b01[:2])]
  transfers between devices with their start and end apart: 8 -> 28, of which waited for: 3 -> 10; matrix products, arithmetic and copies ran while one was open for 27% -> 3% of each run, Pallas kernels for 0% -> 15%
where the time goes in v1:
time: 190 us; the launch traced here: 189 us
  starting transfers between devices  59.7 us (31%)
  Pallas kernels  58.6 us (31%)
  waiting for transfers between devices  42 us (22%)
  blocking collectives  18.7 us (10%)
  other arithmetic  4.6 us (2%)
  local copies, waits for them, and re-layouts  3.52 us (2%)
    ppermute x24, starting transfers between devices, move(): return lax.ppermute(block, ('region', 'sub'), pairs)  55.3 us
    pallas_call x2, Pallas kernels, exchange(): pl.pallas_call(kernel, out_shape=outs, in_specs=[smem] + [any_space] * le...  50.3 us
    ppermute x24, waiting for transfers between devices, move(): return lax.ppermute(block, ('region', 'sub'), pairs)  38.6 us
    unnamed x1, blocking collectives  18.7 us
    pallas_call x1, Pallas kernels, per_device(): pl.pallas_call(planner, out_shape=jax.ShapeDtypeStruct(((N_PAIRS + 1) * L...  8.25 us
    ppermute x4, starting transfers between devices, move(): return lax.ppermute(block, 'region', pairs)  4.39 us
  transfers between devices with their start and end apart: 28, of which 10 were waited for; matrix products, arithmetic and copies ran while one was open for 3% of the time, Pallas kernels for 15%

profile of v1, /device:TPU:0, one launch (start us, length us, event | category | flops | bytes accessed | tf_op | source)
XLA Modules:
  0.0 188.8 jit_solution(6939964264300647995)
XLA Ops:
  0.6 1.6 collective-permute-start.15
  2.3 1.9 %collective-permute-start.14 = (bf16[4,48,2304]{2,1,0:T(8,128)(2,1)}, bf16[4,48,2304]{2,1,0:T(8,128)(2,1)}, u32[]{:S(2)}, u32[]{:S(2)}) collective-permute-start(bf16[4,48,2304]{2,1,0:T(8,128)(2,1)} %refs_9_.2), channel_id=1, source_target_pairs={{0,1},{1,2},{2,3},{3,0},{4,5},{5,6},{6,7},{7,4},{8,9},{9,10},{10,1... | collective-permute-start | bytes 2654216 | tf_op jit(solution)/shard_map/ppermute | solution.py:454
  4.2 1.5 collective-permute-start.1
  5.7 4.3 %collective-permute-start.20 = (bf16[4,48,2304]{2,1,0:T(8,128)(2,1)}, bf16[4,48,2304]{2,1,0:T(8,128)(2,1)S(1)}, u32[]{:S(2)}, u32[]{:S(2)}) collective-permute-start(bf16[4,48,2304]{2,1,0:T(8,128)(2,1)} %refs_9_.2), channel_id=1, source_target_pairs={{0,112},{16,0},{32,16},{48,32},{64,48},{80,64},{96,80},{112,96},{1... | collective-permute-start | bytes 2654216 | tf_op jit(solution)/shard_map/ppermute | solution.py:462
  10.0 0.0 collective-permute-start.6
  10.1 5.1 %collective-permute-done.15.refs_11_ = bf16[4,48,2304]{2,1,0:T(8,128)(2,1)S(1)} collective-permute-done((bf16[4,48,2304]{2,1,0:T(8,128)(2,1)}, bf16[4,48,2304]{2,1,0:T(8,128)(2,1)S(1)}, u32[]{:S(2)}, u32[]{:S(2)}) %collective-permute-start.15) | collective-permute-done | bytes 884768 | tf_op jit(solution)/shard_map/ppermute | solution.py:454
  15.2 2.0 %collective-permute-start = (bf16[4,48,2304]{2,1,0:T(8,128)(2,1)}, bf16[4,48,2304]{2,1,0:T(8,128)(2,1)S(1)}, u32[]{:S(2)}, u32[]{:S(2)}) collective-permute-start(bf16[4,48,2304]{2,1,0:T(8,128)(2,1)} %refs_1_.3), channel_id=1, source_target_pairs={{0,1},{1,2},{2,3},{3,0},{4,5},{5,6},{6,7},{7,4},{8,9},{9,10},{10,1... | collective-permute-start | bytes 2654216 | tf_op jit(solution)/shard_map/ppermute | solution.py:454
  17.3 0.4 collective-permute-done.14.refs_10_
  17.7 1.6 collective-permute-start.17
  19.3 1.0 slice.18
  20.3 4.4 %collective-permute-done.1.refs_3_ = bf16[4,48,2304]{2,1,0:T(8,128)(2,1)S(1)} collective-permute-done((bf16[4,48,2304]{2,1,0:T(8,128)(2,1)}, bf16[4,48,2304]{2,1,0:T(8,128)(2,1)S(1)}, u32[]{:S(2)}, u32[]{:S(2)}) %collective-permute-start.1) | collective-permute-done | bytes 884768 | tf_op jit(solution)/shard_map/ppermute | solution.py:454
  24.7 0.4 collective-permute-start.16
  25.1 2.0 %collective-permute-start.3 = (bf16[2,48,2304]{2,1,0:T(8,128)(2,1)S(1)}, bf16[2,48,2304]{2,1,0:T(8,128)(2,1)S(1)}, u32[]{:S(2)}, u32[]{:S(2)}) collective-permute-start(bf16[2,48,2304]{2,1,0:T(8,128)(2,1)S(1)} %slice.17), channel_id=1, source_target_pairs={{0,1},{1,2},{2,3},{3,0},{4,5},{5,6},{6,7},{7,4},{8,9},{9,10},{10,1... | collective-permute-start | bytes 1327112 | tf_op jit(solution)/shard_map/ppermute | solution.py:454
  27.1 3.3 %collective-permute-done.6.refs_8_ = bf16[4,48,2304]{2,1,0:T(8,128)(2,1)S(1)} collective-permute-done((bf16[4,48,2304]{2,1,0:T(8,128)(2,1)}, bf16[4,48,2304]{2,1,0:T(8,128)(2,1)S(1)}, u32[]{:S(2)}, u32[]{:S(2)}) %collective-permute-start.6) | collective-permute-done | bytes 884768 | tf_op jit(solution)/shard_map/ppermute | solution.py:462
  30.4 0.4 collective-permute-start.18
  30.8 1.4 collective-permute-start.19
  32.2 4.5 %collective-permute-done.17.refs_13_ = bf16[2,48,2304]{2,1,0:T(8,128)(2,1)S(1)} collective-permute-done((bf16[2,48,2304]{2,1,0:T(8,128)(2,1)S(1)}, bf16[2,48,2304]{2,1,0:T(8,128)(2,1)S(1)}, u32[]{:S(2)}, u32[]{:S(2)}) %collective-permute-start.17) | collective-permute-done | bytes 442400 | tf_op jit(solution)/shard_map/ppermute | solution.py:454
  36.8 4.6 %collective-permute-start.4 = (bf16[4,48,2304]{2,1,0:T(8,128)(2,1)S(1)}, bf16[4,48,2304]{2,1,0:T(8,128)(2,1)}, u32[]{:S(2)}, u32[]{:S(2)}) collective-permute-start(bf16[4,48,2304]{2,1,0:T(8,128)(2,1)S(1)} %collective-permute-done.1.refs_3_), channel_id=1, source_target_pairs={{0,3},{1,0},{2,1},{3,2},{4,7},{5,4},{6,5},{7,6},{8,11},{9,8},{10,9... | collective-permute-start | bytes 2654216 | tf_op jit(solution)/shard_map/ppermute | solution.py:454
  41.4 1.4 collective-permute-start.5
  42.8 3.5 %collective-permute-done.3.refs_5_ = bf16[2,48,2304]{2,1,0:T(8,128)(2,1)S(1)} collective-permute-done((bf16[2,48,2304]{2,1,0:T(8,128)(2,1)S(1)}, bf16[2,48,2304]{2,1,0:T(8,128)(2,1)S(1)}, u32[]{:S(2)}, u32[]{:S(2)}) %collective-permute-start.3) | collective-permute-done | bytes 442400 | tf_op jit(solution)/shard_map/ppermute | solution.py:454
  46.3 0.7 copy-done.17
  47.0 0.1 copy.15
  47.2 0.8 reshape.11.refs_2_
  48.0 0.6 dynamic-slice
  49.3 0.2 add_dynamic-update-slice_fusion
  49.5 18.7 %all-reduce.4.refs_1_ = s32[192]{0:T(256)} all-reduce(s32[192]{0:T(256)S(1)} %add_dynamic-update-slice_fusion), channel_id=2, replica_groups=mesh['region'=8,'sub'=16] {'sub'}, use_global_device_ids=true, to_apply=%add.4 | all-reduce | flops 192 | bytes 1536
  68.2 0.6 pad_add_fusion.refs_0_
  68.8 8.3 %plan.1.refs_0_ = s32[520]{0:T(1024)} custom-call(s32[3]{0:T(128)} %pad_add_fusion.refs_0_, s32[192]{0:T(256)} %all-reduce.4.refs_1_, s32[1536]{0:T(1024)} %reshape.11.refs_2_, s32[112]{0:T(128)} %constant.33.clone.refs_3_), custom_call_target="tpu_custom_call" | custom-call | tf_op jit(solution)/shard_map/plan/pallas_call | solution.py:488
  77.2 29.8 %second_application.1 = (f32[4,48,2304]{2,1,0:T(8,128)}, bf16[4,48,2304]{2,1,0:T(8,128)(2,1)}, bf16[4,48,2304]{2,1,0:T(8,128)(2,1)}, bf16[2,48,2304]{2,1,0:T(8,1...) custom-call(s32[520]{0:T(1024)} %plan.1.refs_0_, ...), custom_call_target="tpu_custom_call" | custom-call | flops 20000000000 | bytes 30000000 | tf_op jit(solution)/shard_map/second_application/pallas_call | solution.py:419
  107.0 0.1 collective-permute-start.23
  107.1 10.2 %collective-permute-start.26 = (bf16[2,48,2304]{2,1,0:T(8,128)(2,1)}, bf16[2,48,2304]{2,1,0:T(8,128)(2,1)S(1)}, u32[]{:S(2)}, u32[]{:S(2)}) collective-permute-start(bf16[2,48,2304]{2,1,0:T(8,128)(2,1)} %get-tuple-element.33), channel_id=1, source_target_pairs={{0,3},{1,0},{2,1},{3,2},{4,7},{5,4},{6,5},{7,6},{8,11},{9,8},{10,9... | collective-permute-start | bytes 1327112 | tf_op jit(solution)/shard_map/ppermute | solution.py:454
  117.3 0.1 collective-permute-start.25
  117.4 20.5 %first_application.1 = (f32[4,48,2304]{2,1,0:T(8,128)}, bf16[4,48,2304]{2,1,0:T(8,128)(2,1)}, bf16[4,48,2304]{2,1,0:T(8,128)(2,1)}, bf16[2,48,2304]{2,1,0:T(8,12...) custom-call(s32[520]{0:T(1024)} %plan.1.refs_0_, ...), custom_call_target="tpu_custom_call" | custom-call | flops 10000000000 | bytes 30000000 | tf_op jit(solution)/shard_map/first_application/pallas_call | solution.py:419
  137.9 2.3 %collective-permute-start.9 = (bf16[2,48,2304]{2,1,0:T(8,128)(2,1)}, bf16[2,48,2304]{2,1,0:T(8,128)(2,1)S(1)}, u32[]{:S(2)}, u32[]{:S(2)}) collective-permute-start(bf16[2,48,2304]{2,1,0:T(8,128)(2,1)} %get-tuple-element.22), channel_id=1, source_target_pairs={{0,12},{1,13},{2,14},{3,15},{4,0},{5,1},{6,2},{7,3},{8,4},{9,5},{1... | collective-permute-start | bytes 1327112 | tf_op jit(solution)/shard_map/ppermute | solution.py:454
  140.3 0.3 add_convert_fusion.1
  140.6 9.6 %collective-permute-start.12 = (bf16[2,48,2304]{2,1,0:T(8,128)(2,1)S(1)}, bf16[2,48,2304]{2,1,0:T(8,128)(2,1)S(1)}, u32[]{:S(2)}, u32[]{:S(2)}) collective-permute-start(bf16[2,48,2304]{2,1,0:T(8,128)(2,1)S(1)} %copy-done.20), channel_id=1, source_target_pairs={{0,3},{1,0},{2,1},{3,2},{4,7},{5,4},{6,5},{7,6},{8,11},{9,8},{10,9... | collective-permute-start | bytes 1327112 | tf_op jit(solution)/shard_map/ppermute | solution.py:454
  150.3 0.3 add_convert_fusion
  150.6 0.2 collective-permute-done.9
  150.8 8.4 %collective-permute-start.24 = (bf16[4,48,2304]{2,1,0:T(8,128)(2,1)S(1)}, bf16[4,48,2304]{2,1,0:T(8,128)(2,1)S(1)}, u32[]{:S(2)}, u32[]{:S(2)}) collective-permute-start(bf16[4,48,2304]{2,1,0:T(8,128)(2,1)S(1)} %add_convert_fusion.1), channel_id=1, source_target_pairs={{0,3},{1,0},{2,1},{3,2},{4,7},{5,4},{6,5},{7,6},{8,11},{9,8},{10,9... | collective-permute-start | bytes 2654216 | tf_op jit(solution)/shard_map/ppermute | solution.py:454
  159.1 3.6 %collective-permute-start.27 = (bf16[4,48,2304]{2,1,0:T(8,128)(2,1)S(1)}, bf16[4,48,2304]{2,1,0:T(8,128)(2,1)S(1)}, u32[]{:S(2)}, u32[]{:S(2)}) collective-permute-start(bf16[4,48,2304]{2,1,0:T(8,128)(2,1)S(1)} %add_convert_fusion), channel_id=1, source_target_pairs={{0,12},{1,13},{2,14},{3,15},{4,0},{5,1},{6,2},{7,3},{8,4},{9,5},{1... | collective-permute-start | bytes 2654216 | tf_op jit(solution)/shard_map/ppermute | solution.py:454
  162.7 0.3 add_convert_fusion.3
  163.1 10.9 %collective-permute-done.11 = bf16[4,48,2304]{2,1,0:T(8,128)(2,1)S(1)} collective-permute-done((bf16[4,48,2304]{2,1,0:T(8,128)(2,1)S(1)}, bf16[4,48,2304]{2,1,0:T(8,128)(2,1)S(1)}, u32[]{:S(2)}, u32[]{:S(2)}) %collective-permute-start.11) | collective-permute-done | bytes 884768 | tf_op jit(solution)/shard_map/ppermute | solution.py:454
  174.0 0.3 add_convert_fusion.2
  174.3 2.2 %collective-permute-start.13 = (bf16[4,48,2304]{2,1,0:T(8,128)(2,1)S(1)}, bf16[4,48,2304]{2,1,0:T(8,128)(2,1)S(1)}, u32[]{:S(2)}, u32[]{:S(2)}) collective-permute-start(bf16[4,48,2304]{2,1,0:T(8,128)(2,1)S(1)} %add_convert_fusion.2), channel_id=1, source_target_pairs={{0,12},{1,13},{2,14},{3,15},{4,0},{5,1},{6,2},{7,3},{8,4},{9,5},{1... | collective-permute-start | bytes 2654216 | tf_op jit(solution)/shard_map/ppermute | solution.py:454
  176.5 1.3 negate_convert_fusion
  177.9 9.2 %collective-permute-done.10 = bf16[4,48,2304]{2,1,0:T(8,128)(2,1)S(1)} collective-permute-done((bf16[4,48,2304]{2,1,0:T(8,128)(2,1)S(1)}, bf16[4,48,2304]{2,1,0:T(8,128)(2,1)S(1)}, u32[]{:S(2)}, u32[]{:S(2)}) %collective-permute-start.10) | collective-permute-done | bytes 884768 | tf_op jit(solution)/shard_map/ppermute | solution.py:454
  187.1 0.4 collective-permute-done.13
  187.5 1.3 negate_convert_fusion.1
  (72 shorter events, 0.3 us)
Async XLA Ops:
  0.6 46.4 %copy-start.9 = (s32[512,3]{0,1:T(4,128)S(1)}, s32[512,3]{0,1:T(4,128)}, u32[]{:S(2)}) copy-start(s32[512,3]{0,1:T(4,128)} %param.18) | copy-start | bytes 18436
  0.6 14.5 %collective-permute-start.15 = (bf16[4,48,2304]{2,1,0:T(8,128)(2,1)}, bf16[4,48,2304]{2,1,0:T(8,128)(2,1)S(1)}, u32[]{:S(2)}, u32[]{:S(2)}) collective-permute-start(bf16[4,48,2304]{2,1,0:T(8,128)(2,1)} %refs_9_.2), channel_id=1, source_target_pairs={{0,4},{1,5},{2,6},{3,7},{4,8},{5,9},{6,10},{7,11},{8,12},{9,13},{1... | collective-permute-start | bytes 2654216 | tf_op jit(solution)/shard_map/ppermute | solution.py:454
  2.3 15.4 %collective-permute-start.14 = (bf16[4,48,2304]{2,1,0:T(8,128)(2,1)}, bf16[4,48,2304]{2,1,0:T(8,128)(2,1)}, u32[]{:S(2)}, u32[]{:S(2)}) collective-permute-start(bf16[4,48,2304]{2,1,0:T(8,128)(2,1)} %refs_9_.2), channel_id=1, source_target_pairs={{0,1},{1,2},{2,3},{3,0},{4,5},{5,6},{6,7},{7,4},{8,9},{9,10},{10,1... | collective-permute-start | bytes 2654216 | tf_op jit(solution)/shard_map/ppermute | solution.py:454
  4.2 20.5 %collective-permute-start.1 = (bf16[4,48,2304]{2,1,0:T(8,128)(2,1)}, bf16[4,48,2304]{2,1,0:T(8,128)(2,1)S(1)}, u32[]{:S(2)}, u32[]{:S(2)}) collective-permute-start(bf16[4,48,2304]{2,1,0:T(8,128)(2,1)} %refs_1_.3), channel_id=1, source_target_pairs={{0,4},{1,5},{2,6},{3,7},{4,8},{5,9},{6,10},{7,11},{8,12},{9,13},{1... | collective-permute-start | bytes 2654216 | tf_op jit(solution)/shard_map/ppermute | solution.py:454
  5.7 19.4 %collective-permute-start.20 = (bf16[4,48,2304]{2,1,0:T(8,128)(2,1)}, bf16[4,48,2304]{2,1,0:T(8,128)(2,1)S(1)}, u32[]{:S(2)}, u32[]{:S(2)}) collective-permute-start(bf16[4,48,2304]{2,1,0:T(8,128)(2,1)} %refs_9_.2), channel_id=1, source_target_pairs={{0,112},{16,0},{32,16},{48,32},{64,48},{80,64},{96,80},{112,96},{1... | collective-permute-start | bytes 2654216 | tf_op jit(solution)/shard_map/ppermute | solution.py:462
  10.0 20.4 %collective-permute-start.6 = (bf16[4,48,2304]{2,1,0:T(8,128)(2,1)}, bf16[4,48,2304]{2,1,0:T(8,128)(2,1)S(1)}, u32[]{:S(2)}, u32[]{:S(2)}) collective-permute-start(bf16[4,48,2304]{2,1,0:T(8,128)(2,1)} %refs_1_.3), channel_id=1, source_target_pairs={{0,112},{16,0},{32,16},{48,32},{64,48},{80,64},{96,80},{112,96},{1... | collective-permute-start | bytes 2654216 | tf_op jit(solution)/shard_map/ppermute | solution.py:462
  15.2 27.6 %copy-start.8 = (bf16[4,48,2304]{2,1,0:T(8,128)(2,1)}, bf16[4,48,2304]{2,1,0:T(8,128)(2,1)S(1)}, u32[]{:S(2)}) copy-start(bf16[4,48,2304]{2,1,0:T(8,128)(2,1)S(1)} %collective-permute-done.15.refs_11_) | copy-start | bytes 2654212
  15.2 15.6 %collective-permute-start = (bf16[4,48,2304]{2,1,0:T(8,128)(2,1)}, bf16[4,48,2304]{2,1,0:T(8,128)(2,1)S(1)}, u32[]{:S(2)}, u32[]{:S(2)}) collective-permute-start(bf16[4,48,2304]{2,1,0:T(8,128)(2,1)} %refs_1_.3), channel_id=1, source_target_pairs={{0,1},{1,2},{2,3},{3,0},{4,5},{5,6},{6,7},{7,4},{8,9},{9,10},{10,1... | collective-permute-start | bytes 2654216 | tf_op jit(solution)/shard_map/ppermute | solution.py:454
  17.2 30.8 %copy-start.21 = (u32[128]{0:T(128)S(1)}, u32[128]{0:T(128)}, u32[]{:S(2)}) copy-start(u32[128]{0:T(128)} %constant.49) | copy-start | bytes 1540
  17.2 32.1 %copy-start.10 = (s32[4]{0:T(128)S(1)}, s32[4]{0:T(128)}, u32[]{:S(2)}) copy-start(s32[4]{0:T(128)} %param.17) | copy-start | bytes 52
  17.2 32.0 %copy-start.11 = (s32[4,1]{0,1:T(1,128)S(1)}, s32[4,1]{0,1:T(1,128)}, u32[]{:S(2)}) copy-start(s32[4,1]{0,1:T(1,128)} %param.16) | copy-start | bytes 52
  17.2 32.0 %copy-start.12 = (s32[4]{0:T(128)S(1)}, s32[4]{0:T(128)}, u32[]{:S(2)}) copy-start(s32[4]{0:T(128)} %param.15) | copy-start | bytes 52
  17.7 19.1 %collective-permute-start.17 = (bf16[2,48,2304]{2,1,0:T(8,128)(2,1)S(1)}, bf16[2,48,2304]{2,1,0:T(8,128)(2,1)S(1)}, u32[]{:S(2)}, u32[]{:S(2)}) collective-permute-start(bf16[2,48,2304]{2,1,0:T(8,128)(2,1)S(1)} %slice.19), channel_id=1, source_target_pairs={{0,1},{1,2},{2,3},{3,0},{4,5},{5,6},{6,7},{7,4},{8,9},{9,10},{10,1... | collective-permute-start | bytes 1327112 | tf_op jit(solution)/shard_map/ppermute | solution.py:454
  24.7 52.5 %copy-start.6 = (bf16[4,48,2304]{2,1,0:T(8,128)(2,1)}, bf16[4,48,2304]{2,1,0:T(8,128)(2,1)S(1)}, u32[]{:S(2)}) copy-start(bf16[4,48,2304]{2,1,0:T(8,128)(2,1)S(1)} %collective-permute-done.1.refs_3_) | copy-start | bytes 2654212
  24.7 16.8 %collective-permute-start.16 = (bf16[2,48,2304]{2,1,0:T(8,128)(2,1)S(1)}, bf16[2,48,2304]{2,1,0:T(8,128)(2,1)S(1)}, u32[]{:S(2)}, u32[]{:S(2)}) collective-permute-start(bf16[2,48,2304]{2,1,0:T(8,128)(2,1)S(1)} %slice.18), channel_id=1, source_target_pairs={{0,4},{1,5},{2,6},{3,7},{4,8},{5,9},{6,10},{7,11},{8,12},{9,13},{1... | collective-permute-start | bytes 1327112 | tf_op jit(solution)/shard_map/ppermute | solution.py:454
  25.1 21.2 %copy-start.14 = (bf16[4,48,2304]{2,1,0:T(8,128)(2,1)}, bf16[4,48,2304]{2,1,0:T(8,128)(2,1)S(1)}, u32[]{:S(2)}) copy-start(bf16[4,48,2304]{2,1,0:T(8,128)(2,1)S(1)} %collective-permute-done.20.refs_16_) | copy-start | bytes 2654212
  25.1 21.2 %collective-permute-start.3 = (bf16[2,48,2304]{2,1,0:T(8,128)(2,1)S(1)}, bf16[2,48,2304]{2,1,0:T(8,128)(2,1)S(1)}, u32[]{:S(2)}, u32[]{:S(2)}) collective-permute-start(bf16[2,48,2304]{2,1,0:T(8,128)(2,1)S(1)} %slice.17), channel_id=1, source_target_pairs={{0,1},{1,2},{2,3},{3,0},{4,5},{5,6},{6,7},{7,4},{8,9},{9,10},{10,1... | collective-permute-start | bytes 1327112 | tf_op jit(solution)/shard_map/ppermute | solution.py:454
  30.4 15.9 %copy-start.13 = (bf16[4,48,2304]{2,1,0:T(8,128)(2,1)}, bf16[4,48,2304]{2,1,0:T(8,128)(2,1)S(1)}, u32[]{:S(2)}) copy-start(bf16[4,48,2304]{2,1,0:T(8,128)(2,1)S(1)} %collective-permute-done.6.refs_8_) | copy-start | bytes 2654212
  30.4 46.7 %collective-permute-start.18 = (bf16[4,48,2304]{2,1,0:T(8,128)(2,1)S(1)}, bf16[4,48,2304]{2,1,0:T(8,128)(2,1)}, u32[]{:S(2)}, u32[]{:S(2)}) collective-permute-start(bf16[4,48,2304]{2,1,0:T(8,128)(2,1)S(1)} %collective-permute-done.15.refs_11_), channel_id=1, source_target_pairs={{0,3},{1,0},{2,1},{3,2},{4,7},{5,4},{6,5},{7,6},{8,11},{9,8},{10,9... | collective-permute-start | bytes 2654216 | tf_op jit(solution)/shard_map/ppermute | solution.py:454
  30.8 46.4 %copy-start.7 = (bf16[4,48,2304]{2,1,0:T(8,128)(2,1)}, bf16[4,48,2304]{2,1,0:T(8,128)(2,1)S(1)}, u32[]{:S(2)}) copy-start(bf16[4,48,2304]{2,1,0:T(8,128)(2,1)S(1)} %collective-permute-done.refs_2_) | copy-start | bytes 2654212
  30.8 46.3 %collective-permute-start.19 = (bf16[4,48,2304]{2,1,0:T(8,128)(2,1)}, bf16[4,48,2304]{2,1,0:T(8,128)(2,1)}, u32[]{:S(2)}, u32[]{:S(2)}) collective-permute-start(bf16[4,48,2304]{2,1,0:T(8,128)(2,1)} %collective-permute-done.14.refs_10_), channel_id=1, source_target_pairs={{0,12},{1,13},{2,14},{3,15},{4,0},{5,1},{6,2},{7,3},{8,4},{9,5},{1... | collective-permute-start | bytes 2654216 | tf_op jit(solution)/shard_map/ppermute | solution.py:454
  36.8 9.5 %copy-start.18 = (bf16[2,48,2304]{2,1,0:T(8,128)(2,1)}, bf16[2,48,2304]{2,1,0:T(8,128)(2,1)S(1)}, u32[]{:S(2)}) copy-start(bf16[2,48,2304]{2,1,0:T(8,128)(2,1)S(1)} %collective-permute-done.17.refs_13_) | copy-start | bytes 1327108
  36.8 40.3 %collective-permute-start.4 = (bf16[4,48,2304]{2,1,0:T(8,128)(2,1)S(1)}, bf16[4,48,2304]{2,1,0:T(8,128)(2,1)}, u32[]{:S(2)}, u32[]{:S(2)}) collective-permute-start(bf16[4,48,2304]{2,1,0:T(8,128)(2,1)S(1)} %collective-permute-done.1.refs_3_), channel_id=1, source_target_pairs={{0,3},{1,0},{2,1},{3,2},{4,7},{5,4},{6,5},{7,6},{8,11},{9,8},{10,9... | collective-permute-start | bytes 2654216 | tf_op jit(solution)/shard_map/ppermute | solution.py:454
  41.4 4.9 %copy-start.19 = (bf16[2,48,2304]{2,1,0:T(8,128)(2,1)}, bf16[2,48,2304]{2,1,0:T(8,128)(2,1)S(1)}, u32[]{:S(2)}) copy-start(bf16[2,48,2304]{2,1,0:T(8,128)(2,1)S(1)} %collective-permute-done.16.refs_12_) | copy-start | bytes 1327108
  41.4 35.7 %collective-permute-start.5 = (bf16[4,48,2304]{2,1,0:T(8,128)(2,1)S(1)}, bf16[4,48,2304]{2,1,0:T(8,128)(2,1)}, u32[]{:S(2)}, u32[]{:S(2)}) collective-permute-start(bf16[4,48,2304]{2,1,0:T(8,128)(2,1)S(1)} %collective-permute-done.refs_2_), channel_id=1, source_target_pairs={{0,12},{1,13},{2,14},{3,15},{4,0},{5,1},{6,2},{7,3},{8,4},{9,5},{1... | collective-permute-start | bytes 2654216 | tf_op jit(solution)/shard_map/ppermute | solution.py:454
  46.3 30.8 %collective-permute-start.2 = (bf16[2,48,2304]{2,1,0:T(8,128)(2,1)S(1)}, bf16[2,48,2304]{2,1,0:T(8,128)(2,1)}, u32[]{:S(2)}, u32[]{:S(2)}) collective-permute-start(bf16[2,48,2304]{2,1,0:T(8,128)(2,1)S(1)} %slice.16), channel_id=1, source_target_pairs={{0,4},{1,5},{2,6},{3,7},{4,8},{5,9},{6,10},{7,11},{8,12},{9,13},{1... | collective-permute-start | bytes 1327112 | tf_op jit(solution)/shard_map/ppermute | solution.py:454
  107.0 30.9 %collective-permute-start.23 = (bf16[2,48,2304]{2,1,0:T(8,128)(2,1)}, bf16[2,48,2304]{2,1,0:T(8,128)(2,1)S(1)}, u32[]{:S(2)}, u32[]{:S(2)}) collective-permute-start(bf16[2,48,2304]{2,1,0:T(8,128)(2,1)} %get-tuple-element.30), channel_id=1, source_target_pairs={{0,12},{1,13},{2,14},{3,15},{4,0},{5,1},{6,2},{7,3},{8,4},{9,5},{1... | collective-permute-start | bytes 1327112 | tf_op jit(solution)/shard_map/ppermute | solution.py:454
  107.1 33.5 %collective-permute-start.26 = (bf16[2,48,2304]{2,1,0:T(8,128)(2,1)}, bf16[2,48,2304]{2,1,0:T(8,128)(2,1)S(1)}, u32[]{:S(2)}, u32[]{:S(2)}) collective-permute-start(bf16[2,48,2304]{2,1,0:T(8,128)(2,1)} %get-tuple-element.33), channel_id=1, source_target_pairs={{0,3},{1,0},{2,1},{3,2},{4,7},{5,4},{6,5},{7,6},{8,11},{9,8},{10,9... | collective-permute-start | bytes 1327112 | tf_op jit(solution)/shard_map/ppermute | solution.py:454
  117.3 57.1 %collective-permute-start.21 = (bf16[4,48,2304]{2,1,0:T(8,128)(2,1)}, bf16[4,48,2304]{2,1,0:T(8,128)(2,1)S(1)}, u32[]{:S(2)}, u32[]{:S(2)}) collective-permute-start(bf16[4,48,2304]{2,1,0:T(8,128)(2,1)} %get-tuple-element.27), channel_id=1, source_target_pairs={{0,16},{16,32},{32,48},{48,64},{64,80},{80,96},{96,112},{112,0},{1... | collective-permute-start | bytes 2654216 | tf_op jit(solution)/shard_map/ppermute | solution.py:462
  117.3 23.0 %collective-permute-start.22 = (bf16[4,48,2304]{2,1,0:T(8,128)(2,1)}, bf16[4,48,2304]{2,1,0:T(8,128)(2,1)S(1)}, u32[]{:S(2)}, u32[]{:S(2)}) collective-permute-start(bf16[4,48,2304]{2,1,0:T(8,128)(2,1)} %get-tuple-element.29), channel_id=1, source_target_pairs={{0,4},{1,5},{2,6},{3,7},{4,8},{5,9},{6,10},{7,11},{8,12},{9,13},{1... | collective-permute-start | bytes 2654216 | tf_op jit(solution)/shard_map/ppermute | solution.py:454
  117.3 23.0 %copy-start.5 = (bf16[4,48,2304]{2,1,0:T(8,128)(2,1)S(1)}, bf16[4,48,2304]{2,1,0:T(8,128)(2,1)}, u32[]{:S(2)}) copy-start(bf16[4,48,2304]{2,1,0:T(8,128)(2,1)} %get-tuple-element.28) | copy-start | bytes 2654212
  117.3 32.9 %collective-permute-start.25 = (bf16[4,48,2304]{2,1,0:T(8,128)(2,1)}, bf16[4,48,2304]{2,1,0:T(8,128)(2,1)S(1)}, u32[]{:S(2)}, u32[]{:S(2)}) collective-permute-start(bf16[4,48,2304]{2,1,0:T(8,128)(2,1)} %get-tuple-element.32), channel_id=1, source_target_pairs={{0,1},{1,2},{2,3},{3,0},{4,5},{5,6},{6,7},{7,4},{8,9},{9,10},{10,1... | collective-permute-start | bytes 2654216 | tf_op jit(solution)/shard_map/ppermute | solution.py:454
  137.9 12.3 %copy-start.16 = (bf16[4,48,2304]{2,1,0:T(8,128)(2,1)S(1)}, bf16[4,48,2304]{2,1,0:T(8,128)(2,1)}, u32[]{:S(2)}) copy-start(bf16[4,48,2304]{2,1,0:T(8,128)(2,1)} %get-tuple-element.24) | copy-start | bytes 2654212
  137.9 12.3 %copy-start.3 = (bf16[4,48,2304]{2,1,0:T(8,128)(2,1)S(1)}, bf16[4,48,2304]{2,1,0:T(8,128)(2,1)}, u32[]{:S(2)}) copy-start(bf16[4,48,2304]{2,1,0:T(8,128)(2,1)} %get-tuple-element.31) | copy-start | bytes 2654212
  137.9 12.8 %collective-permute-start.9 = (bf16[2,48,2304]{2,1,0:T(8,128)(2,1)}, bf16[2,48,2304]{2,1,0:T(8,128)(2,1)S(1)}, u32[]{:S(2)}, u32[]{:S(2)}) collective-permute-start(bf16[2,48,2304]{2,1,0:T(8,128)(2,1)} %get-tuple-element.22), channel_id=1, source_target_pairs={{0,12},{1,13},{2,14},{3,15},{4,0},{5,1},{6,2},{7,3},{8,4},{9,5},{1... | collective-permute-start | bytes 1327112 | tf_op jit(solution)/shard_map/ppermute | solution.py:454
  140.3 18.9 %collective-permute-start.8 = (bf16[4,48,2304]{2,1,0:T(8,128)(2,1)}, bf16[4,48,2304]{2,1,0:T(8,128)(2,1)S(1)}, u32[]{:S(2)}, u32[]{:S(2)}) collective-permute-start(bf16[4,48,2304]{2,1,0:T(8,128)(2,1)} %get-tuple-element.21), channel_id=1, source_target_pairs={{0,4},{1,5},{2,6},{3,7},{4,8},{5,9},{6,10},{7,11},{8,12},{9,13},{1... | collective-permute-start | bytes 2654216 | tf_op jit(solution)/shard_map/ppermute | solution.py:454
  140.5 22.2 %copy-start.4 = (bf16[4,48,2304]{2,1,0:T(8,128)(2,1)S(1)}, bf16[4,48,2304]{2,1,0:T(8,128)(2,1)}, u32[]{:S(2)}) copy-start(bf16[4,48,2304]{2,1,0:T(8,128)(2,1)} %get-tuple-element.20) | copy-start | bytes 2654212
  140.6 22.5 %collective-permute-start.12 = (bf16[2,48,2304]{2,1,0:T(8,128)(2,1)S(1)}, bf16[2,48,2304]{2,1,0:T(8,128)(2,1)S(1)}, u32[]{:S(2)}, u32[]{:S(2)}) collective-permute-start(bf16[2,48,2304]{2,1,0:T(8,128)(2,1)S(1)} %copy-done.20), channel_id=1, source_target_pairs={{0,3},{1,0},{2,1},{3,2},{4,7},{5,4},{6,5},{7,6},{8,11},{9,8},{10,9... | collective-permute-start | bytes 1327112 | tf_op jit(solution)/shard_map/ppermute | solution.py:454
  150.2 23.8 %collective-permute-start.11 = (bf16[4,48,2304]{2,1,0:T(8,128)(2,1)S(1)}, bf16[4,48,2304]{2,1,0:T(8,128)(2,1)S(1)}, u32[]{:S(2)}, u32[]{:S(2)}) collective-permute-start(bf16[4,48,2304]{2,1,0:T(8,128)(2,1)S(1)} %copy-done.16), channel_id=1, source_target_pairs={{0,1},{1,2},{2,3},{3,0},{4,5},{5,6},{6,7},{7,4},{8,9},{9,10},{10,1... | collective-permute-start | bytes 2654216 | tf_op jit(solution)/shard_map/ppermute | solution.py:454
  150.5 12.5 %copy-start.15 = (bf16[4,48,2304]{2,1,0:T(8,128)(2,1)S(1)}, bf16[4,48,2304]{2,1,0:T(8,128)(2,1)}, u32[]{:S(2)}) copy-start(bf16[4,48,2304]{2,1,0:T(8,128)(2,1)} %get-tuple-element.19) | copy-start | bytes 2654212
  150.6 23.5 %copy-start.2 = (bf16[4,48,2304]{2,1,0:T(8,128)(2,1)S(1)}, bf16[4,48,2304]{2,1,0:T(8,128)(2,1)}, u32[]{:S(2)}) copy-start(bf16[4,48,2304]{2,1,0:T(8,128)(2,1)} %get-tuple-element.23) | copy-start | bytes 2654212
  150.8 25.8 %collective-permute-start.24 = (bf16[4,48,2304]{2,1,0:T(8,128)(2,1)S(1)}, bf16[4,48,2304]{2,1,0:T(8,128)(2,1)S(1)}, u32[]{:S(2)}, u32[]{:S(2)}) collective-permute-start(bf16[4,48,2304]{2,1,0:T(8,128)(2,1)S(1)} %add_convert_fusion.1), channel_id=1, source_target_pairs={{0,3},{1,0},{2,1},{3,2},{4,7},{5,4},{6,5},{7,6},{8,11},{9,8},{10,9... | collective-permute-start | bytes 2654216 | tf_op jit(solution)/shard_map/ppermute | solution.py:454
  159.1 17.4 %collective-permute-start.27 = (bf16[4,48,2304]{2,1,0:T(8,128)(2,1)S(1)}, bf16[4,48,2304]{2,1,0:T(8,128)(2,1)S(1)}, u32[]{:S(2)}, u32[]{:S(2)}) collective-permute-start(bf16[4,48,2304]{2,1,0:T(8,128)(2,1)S(1)} %add_convert_fusion), channel_id=1, source_target_pairs={{0,12},{1,13},{2,14},{3,15},{4,0},{5,1},{6,2},{7,3},{8,4},{9,5},{1... | collective-permute-start | bytes 2654216 | tf_op jit(solution)/shard_map/ppermute | solution.py:454
  163.0 13.5 %copy-start = (f32[4,48,2304]{2,1,0:T(8,128)S(1)}, f32[4,48,2304]{2,1,0:T(8,128)}, u32[]{:S(2)}) copy-start(f32[4,48,2304]{2,1,0:T(8,128)} %get-tuple-element.26) | copy-start | bytes 5308420
  163.1 14.8 %collective-permute-start.7 = (bf16[4,48,2304]{2,1,0:T(8,128)(2,1)S(1)}, bf16[4,48,2304]{2,1,0:T(8,128)(2,1)S(1)}, u32[]{:S(2)}, u32[]{:S(2)}) collective-permute-start(bf16[4,48,2304]{2,1,0:T(8,128)(2,1)S(1)} %copy-done.15), channel_id=1, source_target_pairs={{0,16},{16,32},{32,48},{48,64},{64,80},{80,96},{96,112},{112,0},{1... | collective-permute-start | bytes 2654216 | tf_op jit(solution)/shard_map/ppermute | solution.py:462
  174.0 13.0 %collective-permute-start.10 = (bf16[4,48,2304]{2,1,0:T(8,128)(2,1)S(1)}, bf16[4,48,2304]{2,1,0:T(8,128)(2,1)S(1)}, u32[]{:S(2)}, u32[]{:S(2)}) collective-permute-start(bf16[4,48,2304]{2,1,0:T(8,128)(2,1)S(1)} %add_convert_fusion.3), channel_id=1, source_target_pairs={{0,3},{1,0},{2,1},{3,2},{4,7},{5,4},{6,5},{7,6},{8,11},{9,8},{10,9... | collective-permute-start | bytes 2654216 | tf_op jit(solution)/shard_map/ppermute | solution.py:454
  174.3 13.1 %collective-permute-start.13 = (bf16[4,48,2304]{2,1,0:T(8,128)(2,1)S(1)}, bf16[4,48,2304]{2,1,0:T(8,128)(2,1)S(1)}, u32[]{:S(2)}, u32[]{:S(2)}) collective-permute-start(bf16[4,48,2304]{2,1,0:T(8,128)(2,1)S(1)} %add_convert_fusion.2), channel_id=1, source_target_pairs={{0,12},{1,13},{2,14},{3,15},{4,0},{5,1},{6,2},{7,3},{8,4},{9,5},{1... | collective-permute-start | bytes 2654216 | tf_op jit(solution)/shard_map/ppermute | solution.py:454
  176.5 10.9 %copy-start.1 = (f32[4,48,2304]{2,1,0:T(8,128)S(1)}, f32[4,48,2304]{2,1,0:T(8,128)}, u32[]{:S(2)}) copy-start(f32[4,48,2304]{2,1,0:T(8,128)} %get-tuple-element.18) | copy-start | bytes 5308420
  (2 other events, 3.5 us)
